TPU v7x, 32 devices: a whole 2x2x4 slice. The times are simulated.
32 devices in a mesh: groups: 2 (over y), vec: 4 (over z), space: 4 (over x, core).
Axes of the slice: x: 2, y: 2, z: 4, core: 2. Of those that a mesh axis runs over, the one named last changes fastest.
Arguments:
- left_vecs: bfloat16 [1024, 4, 3, 4, 2304], P('vec', 'groups', None, 'space'), parts along dimension 1, may hold values from -6 to 6
- right_vecs: bfloat16 [128, 4, 3, 4, 2304], P('vec', 'groups', None, 'space'), parts along dimension 1, may hold values from -6 to 6
- gauge_links: float32 [6, 2, 3, 3, 4, 2304], P('groups', None, None, None, 'space'), parts along dimension 0, may hold values from -2.5 to 2.5
- momenta: int32 [16, 3], replicated, may hold values from -2 to 2
- column_order: int32 [128], replicated, may hold values from 0 to 127, each once
Outputs:
- mesons: float32 [16, 4, 1024, 128], P('space', 'groups', 'vec'), parts along dimension 1
There are 2 independent parts, one for each index of `groups`. A program takes and returns all parts, laid end to end along the dimension named above; an argument that names none is the same for every part. Nothing has to cross between parts.
Inputs may be any that keep to these rules, and one draw needn't show every extreme that they name: `momenta`: each momentum component lies in -2 to 2. `column_order`: a permutation of the right vectors.
All inputs are finite; a program needn't handle non-finite values.
Results may differ from a plain program's by a relative error of at most 0.0039.
Values may be sent and summed in bfloat16 or wider, within the bound.
A program may use at most 192 MiB of HBM per device.

v0:
```python
import math

import jax
import jax.numpy as jnp
from jax import lax
from jax.sharding import PartitionSpec as P

LZ = 48


def with_halo(block, sides, width):
    for axis, dim in sides:
        count = lax.axis_size(axis)
        forward = [(i, i + 1) for i in range(count - 1)]
        forward.append((count - 1, 0))
        backward = [(target, source) for source, target in forward]
        low = lax.ppermute(
            lax.slice_in_dim(block, block.shape[dim] - width, None, axis=dim), axis, forward
        )
        high = lax.ppermute(lax.slice_in_dim(block, 0, width, axis=dim), axis, backward)
        block = jnp.concatenate([low, block, high], axis=dim)
    return block


def from_behind(array, axis, by):
    length = lax.axis_size(axis)
    return lax.ppermute(array, axis, [(i, (i + by) % length) for i in range(length)])


def shifted(field, direction, step, width_z):
    length = field.shape[-1]
    if direction == 1:
        return jnp.roll(field, -step * width_z, axis=-1)
    column = jnp.arange(length) % width_z
    if step == 1:
        return jnp.where(
            column == width_z - 1,
            jnp.roll(field, width_z - 1, axis=-1),
            jnp.roll(field, -1, axis=-1),
        )
    return jnp.where(
        column == 0, jnp.roll(field, 1 - width_z, axis=-1), jnp.roll(field, 1, axis=-1)
    )


def color_mul(matrix, vectors):
    return jnp.sum(matrix[None] * vectors[:, None], axis=2)


def link_apply(link, vectors, adjoint):
    real_part = link[0]
    imag_part = link[1]
    if adjoint:
        real_part = jnp.swapaxes(real_part, 0, 1)
        imag_part = -jnp.swapaxes(imag_part, 0, 1)
    vec_real = vectors[:, 0]
    vec_imag = vectors[:, 1]
    out_real = color_mul(real_part, vec_real) - color_mul(imag_part, vec_imag)
    out_imag = color_mul(real_part, vec_imag) + color_mul(imag_part, vec_real)
    return jnp.stack([out_real, out_imag], axis=1)


def laplace_hops(center, plus_x, minus_x, links, back_x, width_z):
    total = link_apply(links[0], plus_x, False) + link_apply(back_x, minus_x, True)
    for direction in (1, 2):
        total = total + link_apply(links[direction], shifted(center, direction, 1, width_z), False)
        total = total + link_apply(
            shifted(links[direction], direction, -1, width_z),
            shifted(center, direction, -1, width_z),
            True,
        )
    return total - 6.0 * center


def phase_tables(momenta, global_x, count_x, width_y, width_z, length):
    sites = jnp.arange(length)
    coord_y = sites // width_z
    coord_z = sites % width_z
    two_pi = 2.0 * math.pi
    angle_x = jnp.mod(momenta[:, 0:1] * global_x[None], count_x).astype(jnp.float32) * (
        two_pi / count_x
    )
    angle_y = jnp.mod(momenta[:, 1:2] * coord_y[None], width_y).astype(jnp.float32) * (
        two_pi / width_y
    )
    angle_z = jnp.mod(momenta[:, 2:3] * coord_z[None], width_z).astype(jnp.float32) * (
        two_pi / width_z
    )
    angle = angle_x[:, :, None] + (angle_y + angle_z)[:, None, :]
    return (jnp.cos(angle), jnp.sin(angle))


def fold_phase(vectors, cosine, sine):
    values = vectors.astype(jnp.float32)
    vec_real = values[:, 0]
    vec_imag = values[:, 1]
    real_out = vec_real * cosine - vec_imag * sine
    imag_out = -(vec_real * sine + vec_imag * cosine)
    folded = jnp.stack([real_out, imag_out], axis=1).astype(jnp.bfloat16)
    return folded.reshape(folded.shape[0], 2, -1)


def combine_parts(product):
    return jnp.stack(
        [
            product[..., 0, :, 0] - product[..., 1, :, 1],
            product[..., 0, :, 1] + product[..., 1, :, 0],
        ],
        axis=-3,
    )


def contract(folded, stacked):
    product = lax.dot_general(
        folded, stacked, (((folded.ndim - 1,), (2,)), ((), ())), preferred_element_type=jnp.float32
    )
    return combine_parts(product)


def local(left_vecs, right_vecs, gauge_links, momenta, column_order):
    local_x = left_vecs.shape[3]
    plane_size = left_vecs.shape[4]
    space_count = lax.axis_size("space")
    total_x = local_x * space_count
    padded = with_halo(right_vecs, (("space", 3),), 1)
    last_plane = gauge_links[0, :, :, :, local_x - 1 :, :]
    previous = from_behind(last_plane, "space", 1)
    back_x = jnp.concatenate([previous, gauge_links[0, :, :, :, : local_x - 1, :]], axis=3)
    global_x = lax.axis_index("space") * local_x + jnp.arange(local_x)
    cosine, sine = phase_tables(momenta, global_x, total_x, plane_size // LZ, LZ, plane_size)
    folded_all = jax.vmap(fold_phase, in_axes=(None, 0, 0))(left_vecs, cosine, sine)
    fields = padded.astype(jnp.float32)
    center = fields[:, :, :, 1:-1, :]
    smeared = laplace_hops(
        center, fields[:, :, :, 2:, :], fields[:, :, :, :-2, :], gauge_links, back_x, LZ
    ).astype(jnp.bfloat16)
    piece = lax.all_gather(smeared, "vec", axis=0, tiled=True)
    stacked = piece.reshape(piece.shape[0], 2, -1)
    mesons = contract(folded_all, stacked)
    mesons = jnp.take(mesons, column_order, axis=3)
    scale = 1.0 / (8.0 * math.sqrt(3.0 * total_x * plane_size))
    share = lax.psum_scatter(mesons, "space", scatter_dimension=0, tiled=True)
    return share * scale


def solution(mesh):
    in_specs = (
        P("vec", "groups", None, "space", None),
        P("vec", "groups", None, "space", None),
        P("groups", None, None, None, "space", None),
        P(),
        P(),
    )
    out_specs = P("space", "groups", "vec", None)
    return jax.shard_map(local, mesh=mesh, in_specs=in_specs, out_specs=out_specs, check_vma=False)
```

profile of v0, /device:TPU:1, one launch (start us, length us, event | category | flops | bytes accessed | tf_op | source)
XLA Modules:
  0.0 250.4 jit_solution(4806469587797569558)
XLA Ops:
  6.5 1.3 copy.85
  7.9 2.7 %collective-permute-start = (bf16[32,2,3,1,2304]{4,0,2,1,3:T(8,128)(2,1)S(1)}, bf16[32,2,3,1,2304]{4,0,2,1,3:T(8,128)(2,1)S(1)}, u32[]{:S(2)}, u32[]{:S(2)}) collective-permute-start(bf16[32,2,3,1,2304]{4,0,2,1,3:T(8,128)(2,1)S(1)} %copy.85), channel_id=1, source_target_pairs={{0,1},{1,2},{2,3},{3,0},{4,5},{5,6},{6,7},{7,4},{8,9},{9,10},{10,1... | collective-permute-start | bytes 2654216 | tf_op jit(solution)/shard_map/ppermute | solution.py:17
  10.5 1.8 slice_bitcast_fusion.12
  12.3 1.7 collective-permute-start.2
  16.5 9.4 %copy_convert_fusion = f32[256,2,3,1,2304]{4,0,3,2,1:T(8,128)} fusion(bf16[256,2,3,1,2304]{4,1,3,2,0:T(2,128)(2,1)} %param.5), kind=kLoop, calls=%fused_computation.7 | loop fusion | flops 3538944 | bytes 21233664 | tf_op jit(solution)/shard_map/vmap()/convert_element_type | solution.py:94
  25.9 11.8 %slice_bitcast_fusion.1 = (f32[256,3,2304]{2,0,1:T(8,128)}, f32[256,3,2304]{2,0,1:T(8,128)}) fusion(f32[256,2,3,1,2304]{4,0,3,2,1:T(8,128)} %copy_convert_fusion), kind=kLoop, calls=%fused_computation.6 | loop fusion | bytes 28311552 | tf_op jit(solution)/shard_map/vmap()/mul | solution.py:97
  38.3 1.0 copy_bitcast_fusion.2
  40.8 1.0 fusion.34
  44.6 1.0 maximum_select_fusion
  48.7 0.9 multiply_reduce_fusion.11
  51.0 2.9 %multiply_reduce_fusion.19 = (f32[32,3,2304]{2,0,1:T(8,128)S(1)}, f32[32,3,2304]{2,0,1:T(8,128)S(1)}, f32[32,3,2304]{2,0,1:T(8,128)S(1)}, f32[32,3,2304]{2,0,1:T...) fusion(f32[32,3,2304]{2,0,1:T(8,128)S(1)} %get-tuple-element.52, ...), kind=kLoop, calls=%fused_computation.32 | loop fusion | flops 8847360 | bytes 10948608 | tf_op jit(solution)/shard_map/reduce_sum | solution.py:47
  54.4 1.7 fusion.9
  56.2 44.7 %subtract_convert_fusion = (bf16[16,256,1,3,2304]{4,1,3,2,0:T(8,128)(2,1)}, bf16[16,256,1,3,2304]{4,1,3,2,0:T(8,128)(2,1)}) fusion(f32[16,2304]{1,0:T(8,128)S(1)} %get-tuple-element.85, f32[256,3,2304]{2,0,1:T(8,128)} %get-tuple-element.44, f32[16,2304]{1,0:T(8,128)S(1)} %get-tuple-element.84, f32[256,3,2304]{2,0,1:T(8,128)} %get-tuple-element.43), kind=kLoop, calls=%fused_computation.3 | loop fusion | flops 254803968 | bytes 127696896 | tf_op jit(solution)/shard_map/convert
  100.9 25.1 %all-gather.2.cloned.1.call-done = bf16[128,2,3,1,2304]{4,0,2,1,3:T(8,128)(2,1)} async-done(((bf16[32,2,3,1,2304]{4,0,2,1,3:T(8,128)(2,1)}), bf16[128,2,3,1,2304]{4,0,2,1,3:T(8,128)(2,1)}) %all-gather.2.cloned.1.call-update) | async-done | bytes 3538960 | tf_op jit(solution)/shard_map/all_gather | solution.py:137
  126.1 44.3 %fusion.2 = f32[16,256,2,128,2]{3,1,4,2,0:T(8,128)} fusion(bf16[128,2,3,1,2304]{4,0,2,1,3:T(8,128)(2,1)} %all-gather.2.cloned.1.call-done, bf16[16,256,1,3,2304]{4,1,3,2,0:T(8,128)(2,1)} %get-tuple-element.42, bf16[16,256,1,3,2304]{4,1,3,2,0:T(8,128)(2,1)} %get-tuple-element.41), kind=kOutput, calls=%fused_computation.11 | convolution fusion | flops 29217521664 | bytes 125173760 | tf_op jit(solution)/shard_map/dot_general | solution.py:114
  170.4 2.4 fusion.5
  172.8 2.5 fusion.7
  175.3 2.3 pad_maximum_fusion
  177.5 5.5 %copy.96 = f32[16,2,256,128]{2,0,1,3:T(8,128)} copy(f32[16,2,256,128]{3,2,0,1:T(8,128)} %pad_maximum_fusion) | data formatting | bytes 8388608 | tf_op jit(solution)/shard_map/stack | solution.py:104
  183.0 5.1 %gather_fusion = f32[128,16,2,256]{3,1,2,0:T(8,128)} fusion(f32[16,2,256,128]{2,0,1,3:T(8,128)} %copy.96, s32[1024]{0:T(1024)} %pad_clamp_fusion), kind=kCustom, calls=%fused_computation | custom fusion | bytes 8389120 | tf_op jit(solution)/shard_map/jit(_take)/gather | solution.py:140
  188.1 4.5 %select_bitcast_fusion = f32[16,2,256,128]{2,0,1,3:T(8,128)} fusion(f32[128,16,2,256]{3,1,2,0:T(8,128)} %gather_fusion, pred[128]{0:T(512)(128)(4,1)S(1)} %copy-done.3), kind=kLoop, calls=%fused_computation.9 | loop fusion | flops 1048576 | bytes 8388736 | tf_op jit(solution)/shard_map/jit(_take)/select_n | solution.py:140
  192.7 5.3 %copy.97 = f32[16,2,256,128]{3,2,1,0:T(8,128)} copy(f32[16,2,256,128]{2,0,1,3:T(8,128)} %select_bitcast_fusion) | data formatting | bytes 8388608 | tf_op jit(solution)/shard_map/jit(_take)/select_n | solution.py:140
  198.0 43.3 %reduce-scatter.2.cloned.1.call-done = f32[4,2,256,128]{3,2,1,0:T(8,128)} async-done(((f32[16,2,256,128]{3,2,1,0:T(8,128)}), f32[4,2,256,128]{3,2,1,0:T(8,128)}) %reduce-scatter.2.cloned.1.call-update) | async-done | bytes 1048592 | tf_op jit(solution)/shard_map/reduce_scatter | solution.py:142
  241.3 2.3 broadcast_multiply_fusion
  (70 shorter events, 12.1 us)
Async XLA Ops:
  6.5 8.0 %copy-start = (f32[3,2,3,3,1,2304]{5,4,3,2,1,0:T(1,128)S(1)}, f32[3,2,3,3,1,2304]{5,4,3,2,1,0:T(1,128)}, u32[]{:S(2)}) copy-start(f32[3,2,3,3,1,2304]{5,4,3,2,1,0:T(1,128)} %param.7) | copy-start | bytes 1492996
  6.5 8.8 %copy-start.5 = (s32[128]{0:T(128)S(1)}, s32[128]{0:T(128)}, u32[]{:S(2)}) copy-start(s32[128]{0:T(128)} %param.9) | copy-start | bytes 1540
  6.5 10.0 %copy-start.4 = (s32[16,3]{0,1:T(4,128)S(1)}, s32[16,3]{0,1:T(4,128)}, u32[]{:S(2)}) copy-start(s32[16,3]{0,1:T(4,128)} %param.8) | copy-start | bytes 580
  6.5 119.5 %all-gather.2.cloned.1.call-start = ((), (), s32[]{:S(2)}) async-start(), calls=%async_computation.1 | async-start | bytes 4423680 | tf_op jit(solution)/shard_map/all_gather | solution.py:137
  7.9 34.0 %collective-permute-start = (bf16[32,2,3,1,2304]{4,0,2,1,3:T(8,128)(2,1)S(1)}, bf16[32,2,3,1,2304]{4,0,2,1,3:T(8,128)(2,1)S(1)}, u32[]{:S(2)}, u32[]{:S(2)}) collective-permute-start(bf16[32,2,3,1,2304]{4,0,2,1,3:T(8,128)(2,1)S(1)} %copy.85), channel_id=1, source_target_pairs={{0,1},{1,2},{2,3},{3,0},{4,5},{5,6},{6,7},{7,4},{8,9},{9,10},{10,1... | collective-permute-start | bytes 2654216 | tf_op jit(solution)/shard_map/ppermute | solution.py:17
  10.5 31.4 %collective-permute-start.1 = (bf16[32,2,3,1,2304]{4,0,2,1,3:T(8,128)(2,1)S(1)}, bf16[32,2,3,1,2304]{4,0,2,1,3:T(8,128)(2,1)S(1)}, u32[]{:S(2)}, u32[]{:S(2)}) collective-permute-start(bf16[32,2,3,1,2304]{4,0,2,1,3:T(8,128)(2,1)S(1)} %copy.85), channel_id=1, source_target_pairs={{1,0},{2,1},{3,2},{0,3},{5,4},{6,5},{7,6},{4,7},{9,8},{10,9},{11,1... | collective-permute-start | bytes 2654216 | tf_op jit(solution)/shard_map/ppermute | solution.py:20
  12.3 28.5 %collective-permute-start.2 = (f32[2,3,3,1,2304]{4,3,2,1,0:T(1,128)}, f32[2,3,3,1,2304]{4,3,2,1,0:T(1,128)}, u32[]{:S(2)}, u32[]{:S(2)}) collective-permute-start(f32[2,3,3,1,2304]{4,3,2,1,0:T(1,128)} %get-tuple-element.71), channel_id=1, source_target_pairs={{0,1},{1,2},{2,3},{3,0},{4,5},{5,6},{6,7},{7,4},{8,9},{9,10},{10,1... | collective-permute-start | bytes 497672 | tf_op jit(solution)/shard_map/ppermute | solution.py:27
  25.9 11.8 %copy-start.1 = (f32[1,1,3,3,1,2304]{5,4,3,2,1,0:T(1,128)S(1)}, f32[1,1,3,3,1,2304]{5,4,3,2,1,0:T(1,128)}, u32[]{:S(2)}) copy-start(f32[1,1,3,3,1,2304]{5,4,3,2,1,0:T(1,128)} %get-tuple-element.72) | copy-start | bytes 248836
  25.9 11.8 %copy-start.2 = (f32[1,1,3,3,1,2304]{5,4,3,2,1,0:T(1,128)S(1)}, f32[1,1,3,3,1,2304]{5,4,3,2,1,0:T(1,128)}, u32[]{:S(2)}) copy-start(f32[1,1,3,3,1,2304]{5,4,3,2,1,0:T(1,128)} %get-tuple-element.73) | copy-start | bytes 248836
  56.1 185.1 %reduce-scatter.2.cloned.1.call-start = ((), (), s32[]{:S(2)}) async-start(), calls=%async_computation.2 | async-start | bytes 5242880 | tf_op jit(solution)/shard_map/reduce_scatter | solution.py:142
  183.0 5.1 %copy-start.3 = (pred[128]{0:T(512)(128)(4,1)S(1)}, pred[128]{0:T(512)(128)(4,1)}, u32[]{:S(2)}) copy-start(pred[128]{0:T(512)(128)(4,1)} %compare_and_fusion) | copy-start | bytes 388
Sparse Core Ops, SparseCore 0:
  56.3 69.7 all-gather.1
  198.1 43.1 reduce-scatter.1
where the time goes:
time: 252 us; the launch traced here: 250 us
  other arithmetic  83.7 us (33%)
  waiting for transfers between devices  68.5 us (27%)
  matrix products  44.3 us (18%)
  local copies, waits for them, and re-layouts  35.7 us (14%)
  between operations  13.8 us (5%)
  starting transfers between devices  4.44 us (2%)
    another operation x1, other arithmetic  44.7 us
    dot_general x1, matrix products, contract(): lax.dot_general(folded, stacked, (((folded.ndim - 1,), (2,)), ((), ())),...  44.3 us
    reduce_scatter x1, waiting for transfers between devices, local(): share = lax.psum_scatter(mesons, 'space', scatter_dimension=0, tiled=True)  43.3 us
    all_gather x1, waiting for transfers between devices, local(): piece = lax.all_gather(smeared, 'vec', axis=0, tiled=True)  25.1 us
    mul x1, local copies, waits for them, and re-layouts, fold_phase(): real_out = vec_real * cosine - vec_imag * sine  11.8 us
    convert_element_type x1, other arithmetic, fold_phase(): values = vectors.astype(jnp.float32)  9.4 us
    reduce_sum x5, other arithmetic, color_mul(): return jnp.sum(matrix[None] * vectors[:, None], axis=2)  6.36 us
    another operation x1, local copies, waits for them, and re-layouts, combine_parts(): jnp.stack([product[..., 0, :, 0] - product[..., 1, :, 1], product[..., 0,...  5.5 us
  transfers between devices with their start and end apart: 5, of which 2 were waited for; matrix products, arithmetic and copies ran while one was open for 30% of the time, Pallas kernels for 0%

commit v1 on v0

--- a/solution.py
+++ b/solution.py
@@ -3,6 +3,8 @@
 import jax
 import jax.numpy as jnp
 from jax import lax
+from jax.experimental import pallas as pl
+from jax.experimental.pallas import tpu as pltpu
 from jax.sharding import PartitionSpec as P
 
 LZ = 48
@@ -117,7 +119,7 @@
     return combine_parts(product)
 
 
-def local(left_vecs, right_vecs, gauge_links, momenta, column_order):
+def local_plain(left_vecs, right_vecs, gauge_links, momenta, column_order):
     local_x = left_vecs.shape[3]
     plane_size = left_vecs.shape[4]
     space_count = lax.axis_size("space")
@@ -137,10 +139,273 @@
     piece = lax.all_gather(smeared, "vec", axis=0, tiled=True)
     stacked = piece.reshape(piece.shape[0], 2, -1)
     mesons = contract(folded_all, stacked)
-    mesons = jnp.take(mesons, column_order, axis=3)
+    hot = (jnp.arange(column_order.shape[0])[:, None] == column_order[None]).astype(jnp.float32)
+    mesons = jnp.einsum("prij,jk->prik", mesons, hot, precision=lax.Precision.HIGHEST)
     scale = 1.0 / (8.0 * math.sqrt(3.0 * total_x * plane_size))
     share = lax.psum_scatter(mesons, "space", scatter_dimension=0, tiled=True)
     return share * scale
+
+
+ROWS = 16
+TILE = 256
+PIECE = 768
+
+
+def fast_kernel(
+    v_ref, plus_ref, minus_ref, link_ref, back_ref, cos_ref, sin_ref, hot_ref, l_ref, out_ref,
+    hops, moved, gath, both, acc, outbox, own, inbox, total,
+    gsend, grecv, rsend, rrecv,
+):
+    nvec = lax.axis_size("vec")
+    nspace = lax.axis_size("space")
+    vec = lax.axis_index("vec")
+    space = lax.axis_index("space")
+    sites = v_ref.shape[2]
+    chunks = v_ref.shape[1] // ROWS
+    momenta = cos_ref.shape[0]
+    share = momenta // nspace
+    slots = nvec * chunks
+    left = l_ref.shape[0]
+
+    barrier = pltpu.get_barrier_semaphore()
+    for k in range(1, nvec):
+        pl.semaphore_signal(barrier, inc=1, device_id={"vec": lax.rem(vec + k, nvec)},
+                            device_id_type=pl.DeviceIdType.MESH)
+    for k in range(1, nspace):
+        pl.semaphore_signal(barrier, inc=1, device_id={"space": lax.rem(space + k, nspace)},
+                            device_id_type=pl.DeviceIdType.MESH)
+
+    column = lax.rem(lax.broadcasted_iota(jnp.int32, (1, sites), 1), LZ)
+
+    def roll(x, by):
+        return pltpu.roll(x, by % sites, 1)
+
+    def z_up(x):
+        return jnp.where(column == LZ - 1, roll(x, LZ - 1), roll(x, -1))
+
+    def z_down(x):
+        return jnp.where(column == 0, roll(x, 1 - LZ), roll(x, 1))
+
+    hops[0] = link_ref[0]
+    hops[1] = back_ref[...]
+    hops[2] = link_ref[1]
+    hops[3] = roll(link_ref[1], LZ)
+    hops[4] = link_ref[2]
+    hops[5] = z_down(link_ref[2])
+
+    pl.semaphore_wait(barrier, nvec - 1 + nspace - 1)
+
+    def gather_copy(c, k):
+        slot = vec * chunks + c
+        return pltpu.make_async_remote_copy(
+            src_ref=gath.at[slot], dst_ref=gath.at[slot],
+            send_sem=gsend.at[c, k - 1], recv_sem=grecv.at[c, k - 1],
+            device_id={"vec": lax.rem(vec + k, nvec)}, device_id_type=pl.DeviceIdType.MESH)
+
+    def smear(c, carry):
+        rows = pl.ds(pl.multiple_of(c * ROWS, ROWS), ROWS)
+
+        def shift(comp, carry):
+            x = v_ref[comp, rows, :].astype(jnp.float32)
+            moved[0, comp] = plus_ref[comp, rows, :].astype(jnp.float32)
+            moved[1, comp] = minus_ref[comp, rows, :].astype(jnp.float32)
+            moved[2, comp] = roll(x, -LZ)
+            moved[3, comp] = roll(x, LZ)
+            moved[4, comp] = z_up(x)
+            moved[5, comp] = z_down(x)
+            return carry
+
+        lax.fori_loop(0, 6, shift, 0)
+        slot = vec * chunks + c
+
+        def lanes(t, carry):
+            at = pl.multiple_of(t * TILE, TILE)
+            cols = pl.ds(at, TILE)
+            re = [-6.0 * v_ref[2 * a, rows, cols].astype(jnp.float32) for a in range(3)]
+            im = [-6.0 * v_ref[2 * a + 1, rows, cols].astype(jnp.float32) for a in range(3)]
+            for h in range(6):
+                for b in range(3):
+                    vr = moved[h, 2 * b, :, cols]
+                    vi = moved[h, 2 * b + 1, :, cols]
+                    for a in range(3):
+                        row = 3 * a + b if h % 2 == 0 else 3 * b + a
+                        ur = hops[h, row : row + 1, cols]
+                        ui = hops[h, 9 + row : 10 + row, cols]
+                        if h % 2 == 0:
+                            re[a] = re[a] + (ur * vr - ui * vi)
+                            im[a] = im[a] + (ur * vi + ui * vr)
+                        else:
+                            re[a] = re[a] + (ur * vr + ui * vi)
+                            im[a] = im[a] + (ur * vi - ui * vr)
+            for a in range(3):
+                base = 2 * a * sites
+                gath[slot, :, pl.ds(pl.multiple_of(at + base, TILE), TILE)] = re[a].astype(jnp.bfloat16)
+                gath[slot, :, pl.ds(pl.multiple_of(at + base + sites, TILE), TILE)] = im[a].astype(jnp.bfloat16)
+            return carry
+
+        lax.fori_loop(0, sites // TILE, lanes, 0)
+        for k in range(1, nvec):
+            gather_copy(c, k).start()
+        return carry
+
+    lax.fori_loop(0, chunks, smear, 0)
+
+    def reduce_copy(t, k):
+        to = lax.rem(space + k, nspace)
+        return pltpu.make_async_remote_copy(
+            src_ref=outbox.at[t, to], dst_ref=inbox.at[t, k - 1],
+            send_sem=rsend.at[t, k - 1], recv_sem=rrecv.at[t, k - 1],
+            device_id={"space": to}, device_id_type=pl.DeviceIdType.MESH)
+
+    def owner_slot(t):
+        u = t - chunks
+        far = u % (nvec - 1)
+        k = jnp.where(t < chunks, 0, 1 + (2 * far) % (nvec - 1))
+        c = jnp.where(t < chunks, t, u // (nvec - 1))
+        return k, c, lax.rem(vec - k + nvec, nvec) * chunks + c
+
+    block = momenta * ROWS
+
+    def step(t, carry):
+        k, c, slot = owner_slot(t)
+
+        @pl.when(t >= chunks)
+        def _():
+            pltpu.make_async_remote_copy(
+                src_ref=gath.at[slot], dst_ref=gath.at[slot],
+                send_sem=gsend.at[c, k - 1], recv_sem=grecv.at[c, k - 1],
+                device_id={"vec": lax.rem(vec + k, nvec)},
+                device_id_type=pl.DeviceIdType.MESH).wait_recv()
+
+        acc[...] = jnp.zeros_like(acc)
+        parts = sites // PIECE
+
+        def piece(q, carry):
+            colour = q // parts
+            tile = q % parts
+            at = pl.multiple_of(tile * PIECE, PIECE)
+            real_at = pl.multiple_of(colour * 2 * sites + tile * PIECE, PIECE)
+            imag_at = pl.multiple_of(real_at + sites, PIECE)
+            sr = gath[slot, :, pl.ds(real_at, PIECE)].astype(jnp.float32)
+            si = gath[slot, :, pl.ds(imag_at, PIECE)].astype(jnp.float32)
+            for p in range(momenta):
+                cs = cos_ref[p : p + 1, pl.ds(at, PIECE)]
+                sn = sin_ref[p : p + 1, pl.ds(at, PIECE)]
+                both[p * ROWS : (p + 1) * ROWS, :] = (sr * cs + si * sn).astype(jnp.bfloat16)
+                both[block + p * ROWS : block + (p + 1) * ROWS, :] = (si * cs - sr * sn).astype(jnp.bfloat16)
+            dims = (((1,), (1,)), ((), ()))
+            d1 = lax.dot_general(both[...], l_ref[:, pl.ds(real_at, PIECE)], dims,
+                                 preferred_element_type=jnp.float32)
+            d2 = lax.dot_general(both[...], l_ref[:, pl.ds(imag_at, PIECE)], dims,
+                                 preferred_element_type=jnp.float32)
+            acc[0] += d1[:block] + d2[block:]
+            acc[1] += d1[block:] - d2[:block]
+            return carry
+
+        lax.fori_loop(0, 3 * parts, piece, 0)
+        mine = share * ROWS
+        for d in range(nspace):
+            outbox[t, d] = acc[:, d * mine : (d + 1) * mine, :].astype(jnp.bfloat16)
+        own[t] = acc[:, pl.ds(pl.multiple_of(space * mine, mine), mine), :]
+        for m in range(1, nspace):
+            reduce_copy(t, m).start()
+        return carry
+
+    lax.fori_loop(0, slots, step, 0)
+
+    def finish(t, carry):
+        k, c, slot = owner_slot(t)
+        for m in range(1, nspace):
+            reduce_copy(t, m).wait()
+        value = own[t]
+        for m in range(1, nspace):
+            value = value + inbox[t, m - 1].astype(jnp.float32)
+        at = pl.ds(pl.multiple_of(slot * ROWS, ROWS), ROWS)
+        for r in range(2):
+            for p in range(share):
+                total[r, p, at, :] = value[r, p * ROWS : (p + 1) * ROWS, :]
+        return carry
+
+    lax.fori_loop(0, slots, finish, 0)
+    scale = 1.0 / (8.0 * math.sqrt(3.0 * nspace * sites))
+    hot = hot_ref[...]
+    dims = (((0,), (0,)), ((), ()))
+    for r in range(2):
+        for p in range(share):
+            x = total[r, p] * scale
+            high = x.astype(jnp.bfloat16)
+            low = (x - high.astype(jnp.float32)).astype(jnp.bfloat16)
+            out_ref[p, r] = lax.dot_general(
+                high, hot, dims, preferred_element_type=jnp.float32
+            ) + lax.dot_general(low, hot, dims, preferred_element_type=jnp.float32)
+    for c in range(chunks):
+        for k in range(1, nvec):
+            gather_copy(c, k).wait_send()
+
+
+def local_fast(left_vecs, right_vecs, gauge_links, momenta, column_order):
+    left = left_vecs.shape[0]
+    right = right_vecs.shape[0]
+    sites = left_vecs.shape[4]
+    nspace = lax.axis_size("space")
+    nvec = lax.axis_size("vec")
+    count = momenta.shape[0]
+    share = count // nspace
+    chunks = right // ROWS
+    slots = nvec * chunks
+    center = right_vecs.transpose(2, 1, 3, 0, 4).reshape(6, right, sites)
+    plus = from_behind(center, "space", -1)
+    minus = from_behind(center, "space", 1)
+    links = gauge_links.reshape(3, 18, sites)
+    back = from_behind(links[0], "space", 1)
+    rows = left_vecs.transpose(0, 2, 1, 3, 4).reshape(left, 6 * sites)
+    cosine, sine = phase_tables(
+        momenta, lax.axis_index("space")[None], nspace, sites // LZ, LZ, sites
+    )
+    cosine, sine = cosine.reshape(count, sites), sine.reshape(count, sites)
+    hot = (jnp.arange(nvec * right)[:, None] == column_order[None]).astype(jnp.bfloat16)
+    vmem = pl.BlockSpec(memory_space=pltpu.VMEM)
+    mine = share * ROWS
+    return pl.pallas_call(
+        fast_kernel,
+        out_shape=jax.ShapeDtypeStruct((share, 2, left, nvec * right), jnp.float32),
+        in_specs=[vmem] * 9,
+        out_specs=vmem,
+        scratch_shapes=[
+            pltpu.VMEM((6, 18, sites), jnp.float32),
+            pltpu.VMEM((6, 6, ROWS, sites), jnp.float32),
+            pltpu.VMEM((slots, ROWS, 6 * sites), jnp.bfloat16),
+            pltpu.VMEM((2 * count * ROWS, PIECE), jnp.bfloat16),
+            pltpu.VMEM((2, count * ROWS, left), jnp.float32),
+            pltpu.VMEM((slots, nspace, 2, mine, left), jnp.bfloat16),
+            pltpu.VMEM((slots, 2, mine, left), jnp.float32),
+            pltpu.VMEM((slots, nspace - 1, 2, mine, left), jnp.bfloat16),
+            pltpu.VMEM((2, share, nvec * right, left), jnp.float32),
+            pltpu.SemaphoreType.DMA((chunks, nvec - 1)),
+            pltpu.SemaphoreType.DMA((chunks, nvec - 1)),
+            pltpu.SemaphoreType.DMA((slots, nspace - 1)),
+            pltpu.SemaphoreType.DMA((slots, nspace - 1)),
+        ],
+        compiler_params=pltpu.CompilerParams(
+            collective_id=0, has_side_effects=True, vmem_limit_bytes=56 * 1024 * 1024
+        ),
+        cost_estimate=pl.CostEstimate(flops=30_000_000_000, bytes_accessed=20_000_000, transcendentals=0),
+    )(center, plus, minus, links, back, cosine, sine, hot, rows)
+
+
+def local(left_vecs, right_vecs, gauge_links, momenta, column_order):
+    nvec = lax.axis_size("vec")
+    nspace = lax.axis_size("space")
+    fits = (
+        left_vecs.shape[3] == 1
+        and right_vecs.shape[0] % ROWS == 0
+        and nvec == 4
+        and nspace == 4
+        and left_vecs.shape[4] % PIECE == 0
+        and momenta.shape[0] % nspace == 0
+    )
+    chosen = local_fast if fits else local_plain
+    return chosen(left_vecs, right_vecs, gauge_links, momenta, column_order)
 
 
 def solution(mesh):

time: 252 us -> 137 us (0.54)
  the two profiles are of different devices: /device:TPU:1 before, /device:TPU:9 now
where the time goes in v1:
time: 137 us
  Pallas kernels  105 us (77%)
  local copies, waits for them, and re-layouts  22.9 us (17%)
  other arithmetic  5.19 us (4%)
  starting transfers between devices  3.62 us (3%)
    pallas_call x1, Pallas kernels, local_fast(): pl.pallas_call(fast_kernel, out_shape=jax.ShapeDtypeStruct((share, 2, lef...  105 us
    reshape x1, local copies, waits for them, and re-layouts, local_fast(): rows = left_vecs.transpose(0, 2, 1, 3, 4).reshape(left, 6 * sites)  15.1 us
    ppermute x3, starting transfers between devices, from_behind(): lax.ppermute(array, axis, [(i, (i + by) % length) for i in range(length)])  3.62 us
    unnamed x9, local copies, waits for them, and re-layouts  3.28 us
  transfers between devices with their start and end apart: 3, of which 0 were waited for; matrix products, arithmetic and copies ran while one was open for 17% of the time, Pallas kernels for 0%

profile of v1, /device:TPU:9, one launch (start us, length us, event | category | flops | bytes accessed | tf_op | source)
XLA Modules:
  0.0 136.5 jit_solution(70556616611795653)
XLA Ops:
  0.0 1.3 copy.6
  1.3 0.0 copy-start
  1.3 1.8 %collective-permute-start.1 = (bf16[6,32,2304]{2,1,0:T(8,128)(2,1)S(1)}, bf16[6,32,2304]{2,1,0:T(8,128)(2,1)S(1)}, u32[]{:S(2)}, u32[]{:S(2)}) collective-permute-start(bf16[6,32,2304]{2,1,0:T(8,128)(2,1)S(1)} %bitcast.13), channel_id=1, source_target_pairs={{0,1},{1,2},{2,3},{3,0},{4,5},{5,6},{6,7},{7,4},{8,9},{9,10},{10,1... | collective-permute-start | bytes 2654216 | tf_op jit(solution)/shard_map/ppermute | solution.py:29
  3.1 0.0 collective-permute-start
  3.1 1.4 %slice_reduce_fusion = f32[2,3,3,2304]{3,2,1,0:T(4,128)S(1)} fusion(f32[3,2,3,3,1,2304]{5,4,3,2,1,0:T(1,128)} %param.7), kind=kLoop, calls=%fused_computation.2 | loop fusion | bytes 331776 | tf_op jit(solution)/shard_map/slice | solution.py:360
  4.5 0.1 squeeze.3
  4.6 1.8 %collective-permute-start.2 = (f32[18,2304]{1,0:T(8,128)S(1)}, f32[18,2304]{1,0:T(8,128)S(1)}, u32[]{:S(2)}, u32[]{:S(2)}) collective-permute-start(f32[18,2304]{1,0:T(8,128)S(1)} %squeeze.3), channel_id=1, source_target_pairs={{0,1},{1,2},{2,3},{3,0},{4,5},{5,6},{6,7},{7,4},{8,9},{9,10},{10,1... | collective-permute-start | bytes 497672 | tf_op jit(solution)/shard_map/ppermute | solution.py:29
  6.4 0.8 slice_bitcast_fusion.1
  7.2 0.7 fusion.23
  7.9 2.4 %reduce = f32[3,2,3,3,2304]{4,3,2,1,0:T(4,128)S(1)} reduce(f32[3,2,3,3,1,2304]{5,4,3,2,1,0:T(1,128)} %param.7, f32[]{:T(128)} %constant.54), dimensions={4}, to_apply=%param.7.reduce_sub_computation | reduce | bytes 995332 | tf_op args[2]
  10.2 1.1 reshape.103.link_ref
  11.3 15.1 %reshape.104.l_ref = bf16[256,13824]{1,0:T(8,128)(2,1)} reshape(bf16[256,3,2,1,2304]{4,2,3,1,0:T(2,128)(2,1)} %bitcast.11) | data formatting | bytes 14155776 | tf_op jit(solution)/shard_map/reshape | solution.py:361
  26.4 0.0 copy-done
  26.4 1.5 %fusion.11 = (f32[16,2304]{1,0:T(8,128)}, f32[16,2304]{1,0:T(8,128)}) fusion(s32[2304]{0:T(1024)S(1)} %get-tuple-element.9, s32[16]{0:T(128)S(1)} %get-tuple-element.8, s32[2304]{0:T(1024)S(1)} %get-tuple-element.10, s32[16]{0:T(128)S(1)} %get-tuple-element.7, f32[16]{0:T(128)S(1)} %fusion.23), kind=kLoop, calls=%fused_computation.16 | loop fusion | flops 700416 | bytes 313536 | tf_op jit(solution)/shard_map/sin | solution.py:92
  27.9 0.0 copy-done.1
  27.9 0.6 fusion.13.hot_ref
  28.5 0.0 collective-permute-done.2.back_ref
  28.5 0.0 collective-permute-done.1.minus_ref
  28.5 0.0 copy-start.2
  28.5 0.0 collective-permute-done.plus_ref
  28.5 0.7 copy-done.3
  29.2 0.3 copy-done.2
  29.5 104.7 %shard_map.55 = f32[4,2,256,128]{3,2,1,0:T(8,128)} custom-call(bf16[6,32,2304]{2,1,0:T(8,128)(2,1)} %bitcast.15, bf16[6,32,2304]{2,1,0:T(8,128)(2,1)} %collective-permute-done.plus_ref, bf16[6,32,2304]{2,1,0:T(8,128)(2,1)} %copy-done.2, f32[3,18,2304]{2,1,0:T(8,128)} %reshape.103.link_ref, f32[18,2304]{1,0:T(8,128)} %copy-done.3, ...), custom_call_target="tpu_custom_call" | custom-call | flops 30000001024 | bytes 20000000 | tf_op jit(solution)/shard_map/pallas_call | solution.py:369
  134.3 2.3 %copy.10 = f32[4,2,256,128]{3,2,1,0:T(8,128)} copy(f32[4,2,256,128]{3,2,1,0:T(8,128)} %shard_map.55) | data formatting | bytes 2097152
  (3 shorter events, 0.0 us)
Async XLA Ops:
  1.3 25.1 %copy-start = (bf16[3,2,1,32,2304]{4,3,1,0,2:T(8,128)(2,1)}, bf16[3,2,1,32,2304]{4,3,1,0,2:T(8,128)(2,1)S(1)}, u32[]{:S(2)}) copy-start(bf16[3,2,1,32,2304]{4,3,1,0,2:T(8,128)(2,1)S(1)} %copy.6) | copy-start | bytes 2654212
  1.3 27.2 %collective-permute-start.1 = (bf16[6,32,2304]{2,1,0:T(8,128)(2,1)S(1)}, bf16[6,32,2304]{2,1,0:T(8,128)(2,1)S(1)}, u32[]{:S(2)}, u32[]{:S(2)}) collective-permute-start(bf16[6,32,2304]{2,1,0:T(8,128)(2,1)S(1)} %bitcast.13), channel_id=1, source_target_pairs={{0,1},{1,2},{2,3},{3,0},{4,5},{5,6},{6,7},{7,4},{8,9},{9,10},{10,1... | collective-permute-start | bytes 2654216 | tf_op jit(solution)/shard_map/ppermute | solution.py:29
  3.1 25.4 %collective-permute-start = (bf16[6,32,2304]{2,1,0:T(8,128)(2,1)S(1)}, bf16[6,32,2304]{2,1,0:T(8,128)(2,1)}, u32[]{:S(2)}, u32[]{:S(2)}) collective-permute-start(bf16[6,32,2304]{2,1,0:T(8,128)(2,1)S(1)} %bitcast.14), channel_id=1, source_target_pairs={{0,3},{1,0},{2,1},{3,2},{4,7},{5,4},{6,5},{7,6},{8,11},{9,8},{10,9... | collective-permute-start | bytes 2654216 | tf_op jit(solution)/shard_map/ppermute | solution.py:29
  4.6 23.9 %collective-permute-start.2 = (f32[18,2304]{1,0:T(8,128)S(1)}, f32[18,2304]{1,0:T(8,128)S(1)}, u32[]{:S(2)}, u32[]{:S(2)}) collective-permute-start(f32[18,2304]{1,0:T(8,128)S(1)} %squeeze.3), channel_id=1, source_target_pairs={{0,1},{1,2},{2,3},{3,0},{4,5},{5,6},{6,7},{7,4},{8,9},{9,10},{10,1... | collective-permute-start | bytes 497672 | tf_op jit(solution)/shard_map/ppermute | solution.py:29
  11.3 16.6 %copy-start.1 = (s32[128]{0:T(128)S(1)}, s32[128]{0:T(128)}, u32[]{:S(2)}) copy-start(s32[128]{0:T(128)} %param.9) | copy-start | bytes 1540
  28.5 0.7 copy-start.3
  28.5 1.0 copy-start.2

commit v2 on v1

--- a/solution.py
+++ b/solution.py
@@ -195,12 +195,27 @@
 
     pl.semaphore_wait(barrier, nvec - 1 + nspace - 1)
 
-    def gather_copy(c, k):
-        slot = vec * chunks + c
+    def pass_on(slot, way):
         return pltpu.make_async_remote_copy(
             src_ref=gath.at[slot], dst_ref=gath.at[slot],
-            send_sem=gsend.at[c, k - 1], recv_sem=grecv.at[c, k - 1],
-            device_id={"vec": lax.rem(vec + k, nvec)}, device_id_type=pl.DeviceIdType.MESH)
+            send_sem=gsend.at[slot, way], recv_sem=grecv.at[slot],
+            device_id={"vec": lax.rem(vec + (nvec - 1 if way else 1), nvec)},
+            device_id_type=pl.DeviceIdType.MESH)
+
+    def sends_up(source):
+        return jnp.logical_and(source <= vec, vec < nvec - 1)
+
+    def sends_down(source):
+        return jnp.logical_and(source >= vec, vec > 0)
+
+    def send_both(source, slot):
+        @pl.when(sends_up(source))
+        def _():
+            pass_on(slot, 0).start()
+
+        @pl.when(sends_down(source))
+        def _():
+            pass_on(slot, 1).start()
 
     def smear(c, carry):
         rows = pl.ds(pl.multiple_of(c * ROWS, ROWS), ROWS)
@@ -244,8 +259,7 @@
             return carry
 
         lax.fori_loop(0, sites // TILE, lanes, 0)
-        for k in range(1, nvec):
-            gather_copy(c, k).start()
+        send_both(vec, slot)
         return carry
 
     lax.fori_loop(0, chunks, smear, 0)
@@ -259,23 +273,27 @@
 
     def owner_slot(t):
         u = t - chunks
-        far = u % (nvec - 1)
-        k = jnp.where(t < chunks, 0, 1 + (2 * far) % (nvec - 1))
-        c = jnp.where(t < chunks, t, u // (nvec - 1))
-        return k, c, lax.rem(vec - k + nvec, nvec) * chunks + c
+        inner = jnp.logical_and(vec > 0, vec < nvec - 1)
+        toward = jnp.where(2 * vec < nvec, 1, -1)
+        near = jnp.logical_and(inner, u < 2 * chunks)
+        side = jnp.where(u % 2 == 0, toward, -toward)
+        source = vec + jnp.where(
+            near, side, toward * jnp.where(inner, u // chunks, u // chunks + 1)
+        )
+        c = jnp.where(near, u // 2, u % chunks)
+        source = jnp.where(t < chunks, vec, source)
+        c = jnp.where(t < chunks, t, c)
+        return source, source * chunks + c
 
     block = momenta * ROWS
 
     def step(t, carry):
-        k, c, slot = owner_slot(t)
+        source, slot = owner_slot(t)
 
         @pl.when(t >= chunks)
         def _():
-            pltpu.make_async_remote_copy(
-                src_ref=gath.at[slot], dst_ref=gath.at[slot],
-                send_sem=gsend.at[c, k - 1], recv_sem=grecv.at[c, k - 1],
-                device_id={"vec": lax.rem(vec + k, nvec)},
-                device_id_type=pl.DeviceIdType.MESH).wait_recv()
+            pass_on(slot, 0).wait_recv()
+            send_both(source, slot)
 
         acc[...] = jnp.zeros_like(acc)
         parts = sites // PIECE
@@ -314,7 +332,7 @@
     lax.fori_loop(0, slots, step, 0)
 
     def finish(t, carry):
-        k, c, slot = owner_slot(t)
+        source, slot = owner_slot(t)
         for m in range(1, nspace):
             reduce_copy(t, m).wait()
         value = own[t]
@@ -338,9 +356,19 @@
             out_ref[p, r] = lax.dot_general(
                 high, hot, dims, preferred_element_type=jnp.float32
             ) + lax.dot_general(low, hot, dims, preferred_element_type=jnp.float32)
-    for c in range(chunks):
-        for k in range(1, nvec):
-            gather_copy(c, k).wait_send()
+
+    def drain(slot, carry):
+        @pl.when(sends_up(slot // chunks))
+        def _():
+            pass_on(slot, 0).wait_send()
+
+        @pl.when(sends_down(slot // chunks))
+        def _():
+            pass_on(slot, 1).wait_send()
+
+        return carry
+
+    lax.fori_loop(0, slots, drain, 0)
 
 
 def local_fast(left_vecs, right_vecs, gauge_links, momenta, column_order):
@@ -381,8 +409,8 @@
             pltpu.VMEM((slots, 2, mine, left), jnp.float32),
             pltpu.VMEM((slots, nspace - 1, 2, mine, left), jnp.bfloat16),
             pltpu.VMEM((2, share, nvec * right, left), jnp.float32),
-            pltpu.SemaphoreType.DMA((chunks, nvec - 1)),
-            pltpu.SemaphoreType.DMA((chunks, nvec - 1)),
+            pltpu.SemaphoreType.DMA((slots, 2)),
+            pltpu.SemaphoreType.DMA((slots,)),
             pltpu.SemaphoreType.DMA((slots, nspace - 1)),
             pltpu.SemaphoreType.DMA((slots, nspace - 1)),
         ],

time: 137 us -> 115 us (0.84)
  the two profiles are of different devices: /device:TPU:9 before, /device:TPU:1 now
where the time goes in v2:
time: 115 us; the launch traced here: 114 us
  Pallas kernels  81.8 us (71%)
  local copies, waits for them, and re-layouts  22.9 us (20%)
  other arithmetic  5.19 us (5%)
  starting transfers between devices  4.45 us (4%)
    pallas_call x1, Pallas kernels, local_fast(): pl.pallas_call(fast_kernel, out_shape=jax.ShapeDtypeStruct((share, 2, lef...  81.8 us
    reshape x1, local copies, waits for them, and re-layouts, local_fast(): rows = left_vecs.transpose(0, 2, 1, 3, 4).reshape(left, 6 * sites)  15.1 us
    ppermute x3, starting transfers between devices, from_behind(): lax.ppermute(array, axis, [(i, (i + by) % length) for i in range(length)])  4.45 us
    unnamed x9, local copies, waits for them, and re-layouts  3.28 us
    unnamed x1, other arithmetic  2.38 us
  transfers between devices with their start and end apart: 3, of which 0 were waited for; matrix products, arithmetic and copies ran while one was open for 21% of the time, Pallas kernels for 0%

profile of v2, /device:TPU:1, one launch (start us, length us, event | category | flops | bytes accessed | tf_op | source)
XLA Modules:
  0.0 114.4 jit_solution(14834578412094491764)
XLA Ops:
  0.0 1.3 %copy.6 = bf16[3,2,1,32,2304]{4,3,1,0,2:T(8,128)(2,1)S(1)} copy(bf16[3,2,1,32,2304]{4,1,2,0,3:T(2,128)(2,1)} %bitcast.12) | data formatting | bytes 1769472 | tf_op jit(solution)/shard_map/transpose | solution.py:384
  1.3 0.0 copy-start
  1.3 2.7 %collective-permute-start.1 = (bf16[6,32,2304]{2,1,0:T(8,128)(2,1)S(1)}, bf16[6,32,2304]{2,1,0:T(8,128)(2,1)S(1)}, u32[]{:S(2)}, u32[]{:S(2)}) collective-permute-start(bf16[6,32,2304]{2,1,0:T(8,128)(2,1)S(1)} %bitcast.13), channel_id=1, source_target_pairs={{0,1},{1,2},{2,3},{3,0},{4,5},{5,6},{6,7},{7,4},{8,9},{9,10},{10,1... | collective-permute-start | bytes 2654216 | tf_op jit(solution)/shard_map/ppermute | solution.py:29
  3.9 0.0 collective-permute-start
  3.9 1.4 %slice_reduce_fusion = f32[2,3,3,2304]{3,2,1,0:T(4,128)S(1)} fusion(f32[3,2,3,3,1,2304]{5,4,3,2,1,0:T(1,128)} %param.7), kind=kLoop, calls=%fused_computation.2 | loop fusion | bytes 331776 | tf_op jit(solution)/shard_map/slice | solution.py:388
  5.3 0.1 squeeze.3
  5.4 1.8 %collective-permute-start.2 = (f32[18,2304]{1,0:T(8,128)S(1)}, f32[18,2304]{1,0:T(8,128)S(1)}, u32[]{:S(2)}, u32[]{:S(2)}) collective-permute-start(f32[18,2304]{1,0:T(8,128)S(1)} %squeeze.3), channel_id=1, source_target_pairs={{0,1},{1,2},{2,3},{3,0},{4,5},{5,6},{6,7},{7,4},{8,9},{9,10},{10,1... | collective-permute-start | bytes 497672 | tf_op jit(solution)/shard_map/ppermute | solution.py:29
  7.2 0.8 slice_bitcast_fusion.1
  8.0 0.7 fusion.23
  8.7 2.4 %reduce = f32[3,2,3,3,2304]{4,3,2,1,0:T(4,128)S(1)} reduce(f32[3,2,3,3,1,2304]{5,4,3,2,1,0:T(1,128)} %param.7, f32[]{:T(128)} %constant.54), dimensions={4}, to_apply=%param.7.reduce_sub_computation | reduce | bytes 995332 | tf_op args[2]
  11.1 1.1 reshape.103.link_ref
  12.2 15.1 %reshape.104.l_ref = bf16[256,13824]{1,0:T(8,128)(2,1)} reshape(bf16[256,3,2,1,2304]{4,2,3,1,0:T(2,128)(2,1)} %bitcast.11) | data formatting | bytes 14155776 | tf_op jit(solution)/shard_map/reshape | solution.py:389
  27.2 0.0 copy-done
  27.2 1.5 %fusion.11 = (f32[16,2304]{1,0:T(8,128)}, f32[16,2304]{1,0:T(8,128)}) fusion(s32[2304]{0:T(1024)S(1)} %get-tuple-element.9, s32[16]{0:T(128)S(1)} %get-tuple-element.8, s32[2304]{0:T(1024)S(1)} %get-tuple-element.10, s32[16]{0:T(128)S(1)} %get-tuple-element.7, f32[16]{0:T(128)S(1)} %fusion.23), kind=kLoop, calls=%fused_computation.16 | loop fusion | flops 700416 | bytes 313536 | tf_op jit(solution)/shard_map/sin | solution.py:92
  28.7 0.0 copy-done.1
  28.7 0.6 fusion.13.hot_ref
  29.3 0.0 collective-permute-done.2.back_ref
  29.3 0.0 collective-permute-done.1.minus_ref
  29.3 0.0 copy-start.2
  29.4 0.0 collective-permute-done.plus_ref
  29.4 0.7 copy-done.3
  30.0 0.3 copy-done.2
  30.4 81.8 %shard_map.55 = f32[4,2,256,128]{3,2,1,0:T(8,128)} custom-call(bf16[6,32,2304]{2,1,0:T(8,128)(2,1)} %bitcast.15, bf16[6,32,2304]{2,1,0:T(8,128)(2,1)} %collective-permute-done.plus_ref, bf16[6,32,2304]{2,1,0:T(8,128)(2,1)} %copy-done.2, f32[3,18,2304]{2,1,0:T(8,128)} %reshape.103.link_ref, f32[18,2304]{1,0:T(8,128)} %copy-done.3, ...), custom_call_target="tpu_custom_call" | custom-call | flops 30000001024 | bytes 20000000 | tf_op jit(solution)/shard_map/pallas_call | solution.py:397
  112.1 2.3 %copy.10 = f32[4,2,256,128]{3,2,1,0:T(8,128)} copy(f32[4,2,256,128]{3,2,1,0:T(8,128)} %shard_map.55) | data formatting | bytes 2097152
  (3 shorter events, 0.0 us)
Async XLA Ops:
  1.3 26.0 %copy-start = (bf16[3,2,1,32,2304]{4,3,1,0,2:T(8,128)(2,1)}, bf16[3,2,1,32,2304]{4,3,1,0,2:T(8,128)(2,1)S(1)}, u32[]{:S(2)}) copy-start(bf16[3,2,1,32,2304]{4,3,1,0,2:T(8,128)(2,1)S(1)} %copy.6) | copy-start | bytes 2654212
  1.3 28.1 %collective-permute-start.1 = (bf16[6,32,2304]{2,1,0:T(8,128)(2,1)S(1)}, bf16[6,32,2304]{2,1,0:T(8,128)(2,1)S(1)}, u32[]{:S(2)}, u32[]{:S(2)}) collective-permute-start(bf16[6,32,2304]{2,1,0:T(8,128)(2,1)S(1)} %bitcast.13), channel_id=1, source_target_pairs={{0,1},{1,2},{2,3},{3,0},{4,5},{5,6},{6,7},{7,4},{8,9},{9,10},{10,1... | collective-permute-start | bytes 2654216 | tf_op jit(solution)/shard_map/ppermute | solution.py:29
  3.9 25.4 %collective-permute-start = (bf16[6,32,2304]{2,1,0:T(8,128)(2,1)S(1)}, bf16[6,32,2304]{2,1,0:T(8,128)(2,1)}, u32[]{:S(2)}, u32[]{:S(2)}) collective-permute-start(bf16[6,32,2304]{2,1,0:T(8,128)(2,1)S(1)} %bitcast.14), channel_id=1, source_target_pairs={{0,3},{1,0},{2,1},{3,2},{4,7},{5,4},{6,5},{7,6},{8,11},{9,8},{10,9... | collective-permute-start | bytes 2654216 | tf_op jit(solution)/shard_map/ppermute | solution.py:29
  5.4 23.9 %collective-permute-start.2 = (f32[18,2304]{1,0:T(8,128)S(1)}, f32[18,2304]{1,0:T(8,128)S(1)}, u32[]{:S(2)}, u32[]{:S(2)}) collective-permute-start(f32[18,2304]{1,0:T(8,128)S(1)} %squeeze.3), channel_id=1, source_target_pairs={{0,1},{1,2},{2,3},{3,0},{4,5},{5,6},{6,7},{7,4},{8,9},{9,10},{10,1... | collective-permute-start | bytes 497672 | tf_op jit(solution)/shard_map/ppermute | solution.py:29
  12.2 16.6 %copy-start.1 = (s32[128]{0:T(128)S(1)}, s32[128]{0:T(128)}, u32[]{:S(2)}) copy-start(s32[128]{0:T(128)} %param.9) | copy-start | bytes 1540
  29.3 0.7 copy-start.3
  29.3 1.0 copy-start.2

commit v3 on v2

--- a/solution.py
+++ b/solution.py
@@ -186,19 +186,21 @@
     def z_down(x):
         return jnp.where(column == 0, roll(x, 1 - LZ), roll(x, 1))
 
-    hops[0] = link_ref[0]
-    hops[1] = back_ref[...]
-    hops[2] = link_ref[1]
-    hops[3] = roll(link_ref[1], LZ)
-    hops[4] = link_ref[2]
-    hops[5] = z_down(link_ref[2])
+    for row in range(18):
+        hops[1, row : row + 1, :] = back_ref[row]
+        for d in range(3):
+            hops[2 * d, row : row + 1, :] = link_ref[18 * d + row]
+    hops[3] = roll(hops[2], LZ)
+    hops[5] = z_down(hops[4])
 
     pl.semaphore_wait(barrier, nvec - 1 + nspace - 1)
 
-    def pass_on(slot, way):
+    parts = sites // PIECE
+
+    def pass_on(slot, part, way):
         return pltpu.make_async_remote_copy(
-            src_ref=gath.at[slot], dst_ref=gath.at[slot],
-            send_sem=gsend.at[slot, way], recv_sem=grecv.at[slot],
+            src_ref=gath.at[slot, part], dst_ref=gath.at[slot, part],
+            send_sem=gsend.at[slot, part, way], recv_sem=grecv.at[slot, part],
             device_id={"vec": lax.rem(vec + (nvec - 1 if way else 1), nvec)},
             device_id_type=pl.DeviceIdType.MESH)
 
@@ -208,14 +210,14 @@
     def sends_down(source):
         return jnp.logical_and(source >= vec, vec > 0)
 
-    def send_both(source, slot):
+    def send_both(source, slot, part):
         @pl.when(sends_up(source))
         def _():
-            pass_on(slot, 0).start()
+            pass_on(slot, part, 0).start()
 
         @pl.when(sends_down(source))
         def _():
-            pass_on(slot, 1).start()
+            pass_on(slot, part, 1).start()
 
     def smear(c, carry):
         rows = pl.ds(pl.multiple_of(c * ROWS, ROWS), ROWS)
@@ -253,13 +255,18 @@
                             re[a] = re[a] + (ur * vr + ui * vi)
                             im[a] = im[a] + (ur * vi - ui * vr)
             for a in range(3):
-                base = 2 * a * sites
-                gath[slot, :, pl.ds(pl.multiple_of(at + base, TILE), TILE)] = re[a].astype(jnp.bfloat16)
-                gath[slot, :, pl.ds(pl.multiple_of(at + base + sites, TILE), TILE)] = im[a].astype(jnp.bfloat16)
+                part = t // (PIECE // TILE)
+                inside = pl.ds(pl.multiple_of((t % (PIECE // TILE)) * TILE, TILE), TILE)
+                gath[slot, part, 2 * a, :, inside] = re[a].astype(jnp.bfloat16)
+                gath[slot, part, 2 * a + 1, :, inside] = im[a].astype(jnp.bfloat16)
             return carry
 
-        lax.fori_loop(0, sites // TILE, lanes, 0)
-        send_both(vec, slot)
+        def one_part(part, carry):
+            lax.fori_loop(part * (PIECE // TILE), (part + 1) * (PIECE // TILE), lanes, 0)
+            send_both(vec, slot, part)
+            return carry
+
+        lax.fori_loop(0, parts, one_part, 0)
         return carry
 
     lax.fori_loop(0, chunks, smear, 0)
@@ -290,22 +297,22 @@
     def step(t, carry):
         source, slot = owner_slot(t)
 
-        @pl.when(t >= chunks)
-        def _():
-            pass_on(slot, 0).wait_recv()
-            send_both(source, slot)
-
         acc[...] = jnp.zeros_like(acc)
-        parts = sites // PIECE
 
         def piece(q, carry):
-            colour = q // parts
-            tile = q % parts
+            colour = q % 3
+            tile = q // 3
+
+            @pl.when(jnp.logical_and(t >= chunks, colour == 0))
+            def _():
+                pass_on(slot, tile, 0).wait_recv()
+                send_both(source, slot, tile)
+
             at = pl.multiple_of(tile * PIECE, PIECE)
             real_at = pl.multiple_of(colour * 2 * sites + tile * PIECE, PIECE)
             imag_at = pl.multiple_of(real_at + sites, PIECE)
-            sr = gath[slot, :, pl.ds(real_at, PIECE)].astype(jnp.float32)
-            si = gath[slot, :, pl.ds(imag_at, PIECE)].astype(jnp.float32)
+            sr = gath[slot, tile, 2 * colour].astype(jnp.float32)
+            si = gath[slot, tile, 2 * colour + 1].astype(jnp.float32)
             for p in range(momenta):
                 cs = cos_ref[p : p + 1, pl.ds(at, PIECE)]
                 sn = sin_ref[p : p + 1, pl.ds(at, PIECE)]
@@ -327,11 +334,14 @@
         own[t] = acc[:, pl.ds(pl.multiple_of(space * mine, mine), mine), :]
         for m in range(1, nspace):
             reduce_copy(t, m).start()
+
+        @pl.when(t >= 2)
+        def _():
+            finish(t - 2)
+
         return carry
 
-    lax.fori_loop(0, slots, step, 0)
-
-    def finish(t, carry):
+    def finish(t):
         source, slot = owner_slot(t)
         for m in range(1, nspace):
             reduce_copy(t, m).wait()
@@ -342,9 +352,10 @@
         for r in range(2):
             for p in range(share):
                 total[r, p, at, :] = value[r, p * ROWS : (p + 1) * ROWS, :]
-        return carry
-
-    lax.fori_loop(0, slots, finish, 0)
+
+    lax.fori_loop(0, slots, step, 0)
+    finish(slots - 2)
+    finish(slots - 1)
     scale = 1.0 / (8.0 * math.sqrt(3.0 * nspace * sites))
     hot = hot_ref[...]
     dims = (((0,), (0,)), ((), ()))
@@ -357,18 +368,21 @@
                 high, hot, dims, preferred_element_type=jnp.float32
             ) + lax.dot_general(low, hot, dims, preferred_element_type=jnp.float32)
 
-    def drain(slot, carry):
+    def drain(n, carry):
+        slot = n // parts
+        part = n % parts
+
         @pl.when(sends_up(slot // chunks))
         def _():
-            pass_on(slot, 0).wait_send()
+            pass_on(slot, part, 0).wait_send()
 
         @pl.when(sends_down(slot // chunks))
         def _():
-            pass_on(slot, 1).wait_send()
+            pass_on(slot, part, 1).wait_send()
 
         return carry
 
-    lax.fori_loop(0, slots, drain, 0)
+    lax.fori_loop(0, slots * parts, drain, 0)
 
 
 def local_fast(left_vecs, right_vecs, gauge_links, momenta, column_order):
@@ -384,8 +398,8 @@
     center = right_vecs.transpose(2, 1, 3, 0, 4).reshape(6, right, sites)
     plus = from_behind(center, "space", -1)
     minus = from_behind(center, "space", 1)
-    links = gauge_links.reshape(3, 18, sites)
-    back = from_behind(links[0], "space", 1)
+    links = gauge_links.reshape(54, 1, sites)
+    back = from_behind(links[:18], "space", 1)
     rows = left_vecs.transpose(0, 2, 1, 3, 4).reshape(left, 6 * sites)
     cosine, sine = phase_tables(
         momenta, lax.axis_index("space")[None], nspace, sites // LZ, LZ, sites
@@ -402,15 +416,15 @@
         scratch_shapes=[
             pltpu.VMEM((6, 18, sites), jnp.float32),
             pltpu.VMEM((6, 6, ROWS, sites), jnp.float32),
-            pltpu.VMEM((slots, ROWS, 6 * sites), jnp.bfloat16),
+            pltpu.VMEM((slots, sites // PIECE, 6, ROWS, PIECE), jnp.bfloat16),
             pltpu.VMEM((2 * count * ROWS, PIECE), jnp.bfloat16),
             pltpu.VMEM((2, count * ROWS, left), jnp.float32),
             pltpu.VMEM((slots, nspace, 2, mine, left), jnp.bfloat16),
             pltpu.VMEM((slots, 2, mine, left), jnp.float32),
             pltpu.VMEM((slots, nspace - 1, 2, mine, left), jnp.bfloat16),
             pltpu.VMEM((2, share, nvec * right, left), jnp.float32),
-            pltpu.SemaphoreType.DMA((slots, 2)),
-            pltpu.SemaphoreType.DMA((slots,)),
+            pltpu.SemaphoreType.DMA((slots, sites // PIECE, 2)),
+            pltpu.SemaphoreType.DMA((slots, sites // PIECE)),
             pltpu.SemaphoreType.DMA((slots, nspace - 1)),
             pltpu.SemaphoreType.DMA((slots, nspace - 1)),
         ],

time: 115 us -> 111 us (0.965)
  other arithmetic: 5.19 us -> 2.8 us
  local copies, waits for them, and re-layouts: 22.9 us -> 21.6 us
    unnamed x1 -> x0, other arithmetic: 2.38 us -> none
    unnamed x9 -> x11, local copies, waits for them, and re-layouts: 3.28 us -> 3.6 us
  transfers between devices with their start and end apart: 3 -> 3, of which waited for: 0 -> 0; matrix products, arithmetic and copies ran while one was open for 21% -> 18% of each run, Pallas kernels for 0% -> 0%
where the time goes in v3:
time: 111 us; the launch traced here: 110 us
  Pallas kernels  81.4 us (73%)
  local copies, waits for them, and re-layouts  21.6 us (19%)
  starting transfers between devices  4.45 us (4%)
  other arithmetic  2.8 us (3%)
    pallas_call x1, Pallas kernels, local_fast(): pl.pallas_call(fast_kernel, out_shape=jax.ShapeDtypeStruct((share, 2, lef...  81.4 us
    reshape x1, local copies, waits for them, and re-layouts, local_fast(): rows = left_vecs.transpose(0, 2, 1, 3, 4).reshape(left, 6 * sites)  15.1 us
    ppermute x3, starting transfers between devices, from_behind(): lax.ppermute(array, axis, [(i, (i + by) % length) for i in range(length)])  4.45 us
    unnamed x11, local copies, waits for them, and re-layouts  3.6 us
  transfers between devices with their start and end apart: 3, of which 0 were waited for; matrix products, arithmetic and copies ran while one was open for 18% of the time, Pallas kernels for 0%

profile of v3, /device:TPU:1, one launch (start us, length us, event | category | flops | bytes accessed | tf_op | source)
XLA Modules:
  0.0 110.3 jit_solution(2406719422339632273)
XLA Ops:
  0.0 1.3 %copy.6 = bf16[3,2,1,32,2304]{4,3,1,0,2:T(8,128)(2,1)S(1)} copy(bf16[3,2,1,32,2304]{4,1,2,0,3:T(2,128)(2,1)} %bitcast.14) | data formatting | bytes 1769472 | tf_op jit(solution)/shard_map/transpose | solution.py:398
  1.3 0.0 copy-start
  1.3 2.7 %collective-permute-start.1 = (bf16[6,32,2304]{2,1,0:T(8,128)(2,1)S(1)}, bf16[6,32,2304]{2,1,0:T(8,128)(2,1)S(1)}, u32[]{:S(2)}, u32[]{:S(2)}) collective-permute-start(bf16[6,32,2304]{2,1,0:T(8,128)(2,1)S(1)} %bitcast.15), channel_id=1, source_target_pairs={{0,1},{1,2},{2,3},{3,0},{4,5},{5,6},{6,7},{7,4},{8,9},{9,10},{10,1... | collective-permute-start | bytes 2654216 | tf_op jit(solution)/shard_map/ppermute | solution.py:29
  3.9 0.0 collective-permute-start
  3.9 0.9 slice.15
  4.9 1.8 %collective-permute-start.2 = (f32[18,1,2304]{2,1,0:T(1,128)S(1)}, f32[18,1,2304]{2,1,0:T(1,128)S(1)}, u32[]{:S(2)}, u32[]{:S(2)}) collective-permute-start(f32[18,1,2304]{2,1,0:T(1,128)S(1)} %bitcast.18), channel_id=1, source_target_pairs={{0,1},{1,2},{2,3},{3,0},{4,5},{5,6},{6,7},{7,4},{8,9},{9,10},{10,1... | collective-permute-start | bytes 497672 | tf_op jit(solution)/shard_map/ppermute | solution.py:29
  6.7 0.8 slice_bitcast_fusion.1
  7.4 0.7 fusion.23
  8.1 0.0 copy-start.1
  8.1 15.1 %reshape.103.l_ref = bf16[256,13824]{1,0:T(8,128)(2,1)} reshape(bf16[256,3,2,1,2304]{4,2,3,1,0:T(2,128)(2,1)} %bitcast.13) | data formatting | bytes 14155776 | tf_op jit(solution)/shard_map/reshape | solution.py:403
  23.2 0.0 copy-done
  23.2 1.5 %fusion.11 = (f32[16,2304]{1,0:T(8,128)}, f32[16,2304]{1,0:T(8,128)}) fusion(s32[2304]{0:T(1024)S(1)} %get-tuple-element.9, s32[16]{0:T(128)S(1)} %get-tuple-element.8, s32[2304]{0:T(1024)S(1)} %get-tuple-element.10, s32[16]{0:T(128)S(1)} %get-tuple-element.7, f32[16]{0:T(128)S(1)} %fusion.23), kind=kLoop, calls=%fused_computation.15 | loop fusion | flops 700416 | bytes 313536 | tf_op jit(solution)/shard_map/sin | solution.py:92
  24.7 0.0 copy-done.1
  24.7 0.6 fusion.13.hot_ref
  25.3 0.0 collective-permute-done.2.back_ref
  25.3 0.0 collective-permute-done.1.minus_ref
  25.3 0.0 copy-start.2
  25.3 0.0 collective-permute-done.plus_ref
  25.3 0.0 copy-start.3
  25.3 0.6 copy-done.4
  26.0 0.3 copy-done.2
  26.3 0.4 copy-done.3
  26.6 81.4 %shard_map.55 = f32[4,2,256,128]{3,2,1,0:T(8,128)} custom-call(bf16[6,32,2304]{2,1,0:T(8,128)(2,1)} %bitcast.17, bf16[6,32,2304]{2,1,0:T(8,128)(2,1)} %copy-done.3, bf16[6,32,2304]{2,1,0:T(8,128)(2,1)} %copy-done.2, f32[54,1,2304]{2,1,0:T(1,128)} %bitcast.19, f32[18,1,2304]{2,1,0:T(1,128)} %copy-done.4, f32[16,2304]{1,0:T(8,128)} %get-tuple-element.6.cos_ref, ...), custom_call_target="tpu_custom_call" | custom-call | flops 30000001024 | bytes 20000000 | tf_op jit(solution)/shard_map/pallas_call | solution.py:411
  108.1 2.3 %copy.8 = f32[4,2,256,128]{3,2,1,0:T(8,128)} copy(f32[4,2,256,128]{3,2,1,0:T(8,128)} %shard_map.55) | data formatting | bytes 2097152
  (2 shorter events, 0.0 us)
Async XLA Ops:
  1.3 21.9 %copy-start = (bf16[3,2,1,32,2304]{4,3,1,0,2:T(8,128)(2,1)}, bf16[3,2,1,32,2304]{4,3,1,0,2:T(8,128)(2,1)S(1)}, u32[]{:S(2)}) copy-start(bf16[3,2,1,32,2304]{4,3,1,0,2:T(8,128)(2,1)S(1)} %copy.6) | copy-start | bytes 2654212
  1.3 24.0 %collective-permute-start.1 = (bf16[6,32,2304]{2,1,0:T(8,128)(2,1)S(1)}, bf16[6,32,2304]{2,1,0:T(8,128)(2,1)S(1)}, u32[]{:S(2)}, u32[]{:S(2)}) collective-permute-start(bf16[6,32,2304]{2,1,0:T(8,128)(2,1)S(1)} %bitcast.15), channel_id=1, source_target_pairs={{0,1},{1,2},{2,3},{3,0},{4,5},{5,6},{6,7},{7,4},{8,9},{9,10},{10,1... | collective-permute-start | bytes 2654216 | tf_op jit(solution)/shard_map/ppermute | solution.py:29
  3.9 21.4 %collective-permute-start = (bf16[6,32,2304]{2,1,0:T(8,128)(2,1)S(1)}, bf16[6,32,2304]{2,1,0:T(8,128)(2,1)S(1)}, u32[]{:S(2)}, u32[]{:S(2)}) collective-permute-start(bf16[6,32,2304]{2,1,0:T(8,128)(2,1)S(1)} %bitcast.16), channel_id=1, source_target_pairs={{0,3},{1,0},{2,1},{3,2},{4,7},{5,4},{6,5},{7,6},{8,11},{9,8},{10,9... | collective-permute-start | bytes 2654216 | tf_op jit(solution)/shard_map/ppermute | solution.py:29
  4.9 20.4 %collective-permute-start.2 = (f32[18,1,2304]{2,1,0:T(1,128)S(1)}, f32[18,1,2304]{2,1,0:T(1,128)S(1)}, u32[]{:S(2)}, u32[]{:S(2)}) collective-permute-start(f32[18,1,2304]{2,1,0:T(1,128)S(1)} %bitcast.18), channel_id=1, source_target_pairs={{0,1},{1,2},{2,3},{3,0},{4,5},{5,6},{6,7},{7,4},{8,9},{9,10},{10,1... | collective-permute-start | bytes 497672 | tf_op jit(solution)/shard_map/ppermute | solution.py:29
  8.1 16.6 %copy-start.1 = (s32[128]{0:T(128)S(1)}, s32[128]{0:T(128)}, u32[]{:S(2)}) copy-start(s32[128]{0:T(128)} %param.9) | copy-start | bytes 1540
  25.3 0.7 copy-start.4
  25.3 1.0 copy-start.2
  25.3 1.3 %copy-start.3 = (bf16[6,32,2304]{2,1,0:T(8,128)(2,1)}, bf16[6,32,2304]{2,1,0:T(8,128)(2,1)S(1)}, u32[]{:S(2)}) copy-start(bf16[6,32,2304]{2,1,0:T(8,128)(2,1)S(1)} %collective-permute-done.plus_ref) | copy-start | bytes 2654212

commit v4 on v3

--- a/solution.py
+++ b/solution.py
@@ -152,8 +152,8 @@
 
 
 def fast_kernel(
-    v_ref, plus_ref, minus_ref, link_ref, back_ref, cos_ref, sin_ref, hot_ref, l_ref, out_ref,
-    hops, moved, gath, both, acc, outbox, own, inbox, total,
+    v_ref, plus_ref, minus_ref, link_ref, back_ref, cos_ref, sin_ref, l_ref, total,
+    hops, moved, gath, both, acc, outbox, own, inbox,
     gsend, grecv, rsend, rrecv,
 ):
     nvec = lax.axis_size("vec")
@@ -224,12 +224,10 @@
 
         def shift(comp, carry):
             x = v_ref[comp, rows, :].astype(jnp.float32)
-            moved[0, comp] = plus_ref[comp, rows, :].astype(jnp.float32)
-            moved[1, comp] = minus_ref[comp, rows, :].astype(jnp.float32)
-            moved[2, comp] = roll(x, -LZ)
-            moved[3, comp] = roll(x, LZ)
-            moved[4, comp] = z_up(x)
-            moved[5, comp] = z_down(x)
+            moved[0, comp] = roll(x, -LZ)
+            moved[1, comp] = roll(x, LZ)
+            moved[2, comp] = z_up(x)
+            moved[3, comp] = z_down(x)
             return carry
 
         lax.fori_loop(0, 6, shift, 0)
@@ -242,8 +240,13 @@
             im = [-6.0 * v_ref[2 * a + 1, rows, cols].astype(jnp.float32) for a in range(3)]
             for h in range(6):
                 for b in range(3):
-                    vr = moved[h, 2 * b, :, cols]
-                    vi = moved[h, 2 * b + 1, :, cols]
+                    if h < 2:
+                        halo = minus_ref if h else plus_ref
+                        vr = halo[2 * b, rows, cols].astype(jnp.float32)
+                        vi = halo[2 * b + 1, rows, cols].astype(jnp.float32)
+                    else:
+                        vr = moved[h - 2, 2 * b, :, cols]
+                        vi = moved[h - 2, 2 * b + 1, :, cols]
                     for a in range(3):
                         row = 3 * a + b if h % 2 == 0 else 3 * b + a
                         ur = hops[h, row : row + 1, cols]
@@ -356,33 +359,35 @@
     lax.fori_loop(0, slots, step, 0)
     finish(slots - 2)
     finish(slots - 1)
-    scale = 1.0 / (8.0 * math.sqrt(3.0 * nspace * sites))
+
+    def drain(n, carry):
+        slot = n // parts
+        part = n % parts
+
+        @pl.when(sends_up(slot // chunks))
+        def _():
+            pass_on(slot, part, 0).wait_send()
+
+        @pl.when(sends_down(slot // chunks))
+        def _():
+            pass_on(slot, part, 1).wait_send()
+
+        return carry
+
+    lax.fori_loop(0, slots * parts, drain, 0)
+
+
+def turn_kernel(scale, total_ref, hot_ref, out_ref):
     hot = hot_ref[...]
     dims = (((0,), (0,)), ((), ()))
     for r in range(2):
-        for p in range(share):
-            x = total[r, p] * scale
+        for p in range(out_ref.shape[0]):
+            x = total_ref[r, p] * scale
             high = x.astype(jnp.bfloat16)
             low = (x - high.astype(jnp.float32)).astype(jnp.bfloat16)
             out_ref[p, r] = lax.dot_general(
                 high, hot, dims, preferred_element_type=jnp.float32
             ) + lax.dot_general(low, hot, dims, preferred_element_type=jnp.float32)
-
-    def drain(n, carry):
-        slot = n // parts
-        part = n % parts
-
-        @pl.when(sends_up(slot // chunks))
-        def _():
-            pass_on(slot, part, 0).wait_send()
-
-        @pl.when(sends_down(slot // chunks))
-        def _():
-            pass_on(slot, part, 1).wait_send()
-
-        return carry
-
-    lax.fori_loop(0, slots * parts, drain, 0)
 
 
 def local_fast(left_vecs, right_vecs, gauge_links, momenta, column_order):
@@ -408,21 +413,20 @@
     hot = (jnp.arange(nvec * right)[:, None] == column_order[None]).astype(jnp.bfloat16)
     vmem = pl.BlockSpec(memory_space=pltpu.VMEM)
     mine = share * ROWS
-    return pl.pallas_call(
+    total = pl.pallas_call(
         fast_kernel,
-        out_shape=jax.ShapeDtypeStruct((share, 2, left, nvec * right), jnp.float32),
-        in_specs=[vmem] * 9,
+        out_shape=jax.ShapeDtypeStruct((2, share, nvec * right, left), jnp.float32),
+        in_specs=[vmem] * 8,
         out_specs=vmem,
         scratch_shapes=[
             pltpu.VMEM((6, 18, sites), jnp.float32),
-            pltpu.VMEM((6, 6, ROWS, sites), jnp.float32),
+            pltpu.VMEM((4, 6, ROWS, sites), jnp.float32),
             pltpu.VMEM((slots, sites // PIECE, 6, ROWS, PIECE), jnp.bfloat16),
             pltpu.VMEM((2 * count * ROWS, PIECE), jnp.bfloat16),
             pltpu.VMEM((2, count * ROWS, left), jnp.float32),
             pltpu.VMEM((slots, nspace, 2, mine, left), jnp.bfloat16),
             pltpu.VMEM((slots, 2, mine, left), jnp.float32),
             pltpu.VMEM((slots, nspace - 1, 2, mine, left), jnp.bfloat16),
-            pltpu.VMEM((2, share, nvec * right, left), jnp.float32),
             pltpu.SemaphoreType.DMA((slots, sites // PIECE, 2)),
             pltpu.SemaphoreType.DMA((slots, sites // PIECE)),
             pltpu.SemaphoreType.DMA((slots, nspace - 1)),
@@ -432,7 +436,15 @@
             collective_id=0, has_side_effects=True, vmem_limit_bytes=56 * 1024 * 1024
         ),
         cost_estimate=pl.CostEstimate(flops=30_000_000_000, bytes_accessed=20_000_000, transcendentals=0),
-    )(center, plus, minus, links, back, cosine, sine, hot, rows)
+    )(center, plus, minus, links, back, cosine, sine, rows)
+    scale = 1.0 / (8.0 * math.sqrt(3.0 * nspace * sites))
+    return pl.pallas_call(
+        lambda *refs: turn_kernel(scale, *refs),
+        out_shape=jax.ShapeDtypeStruct((share, 2, left, nvec * right), jnp.float32),
+        in_specs=[vmem] * 2,
+        out_specs=vmem,
+        compiler_params=pltpu.CompilerParams(vmem_limit_bytes=16 * 1024 * 1024),
+    )(total, hot)
 
 
 def local(left_vecs, right_vecs, gauge_links, momenta, column_order):

time: 111 us -> 111 us (level)
  waiting for transfers between devices: 0.01 us -> 1.72 us
  starting transfers between devices: 4.45 us -> 3.21 us
    ppermute x3, waiting for transfers between devices: 0.01 us -> 1.72 us  [from_behind(): lax.ppermute(array, axis, [(i, (i + by) % length) for i in range(length)])]
    ppermute x3, starting transfers between devices: 4.45 us -> 3.21 us  [from_behind(): lax.ppermute(array, axis, [(i, (i + by) % length) for i in range(length)])]
    unnamed x11 -> x12, local copies, waits for them, and re-layouts: 3.6 us -> 2.57 us
    pallas_call x1 -> x2, Pallas kernels: 81.4 us -> 82.4 us  [the longest x1 81 us: local_fast(): pl.pallas_call(fast_kernel, out_shape=jax.ShapeDtypeStruct((2, share, nve...]
  transfers between devices with their start and end apart: 3 -> 3, of which waited for: 0 -> 1; matrix products, arithmetic and copies ran while one was open for 18% -> 17% of each run, Pallas kernels for 0% -> 0%
where the time goes in v4:
time: 111 us; the launch traced here: 110 us
  Pallas kernels  82.4 us (74%)
  local copies, waits for them, and re-layouts  20.6 us (19%)
  starting transfers between devices  3.21 us (3%)
  other arithmetic  2.19 us (2%)
  waiting for transfers between devices  1.72 us (2%)
    pallas_call x1, Pallas kernels, local_fast(): pl.pallas_call(fast_kernel, out_shape=jax.ShapeDtypeStruct((2, share, nve...  81 us
    reshape x1, local copies, waits for them, and re-layouts, local_fast(): rows = left_vecs.transpose(0, 2, 1, 3, 4).reshape(left, 6 * sites)  15.1 us
    ppermute x3, starting transfers between devices, from_behind(): lax.ppermute(array, axis, [(i, (i + by) % length) for i in range(length)])  3.21 us
    unnamed x12, local copies, waits for them, and re-layouts  2.57 us
  transfers between devices with their start and end apart: 3, of which 1 were waited for; matrix products, arithmetic and copies ran while one was open for 17% of the time, Pallas kernels for 0%

profile of v4, /device:TPU:1, one launch (start us, length us, event | category | flops | bytes accessed | tf_op | source)
XLA Modules:
  0.0 110.2 jit_solution(13435724944289143058)
XLA Ops:
  0.0 1.3 %copy.6 = bf16[3,2,1,32,2304]{4,3,1,0,2:T(8,128)(2,1)S(1)} copy(bf16[3,2,1,32,2304]{4,1,2,0,3:T(2,128)(2,1)} %bitcast.14) | data formatting | bytes 1769472 | tf_op jit(solution)/shard_map/transpose | solution.py:403
  1.3 0.0 copy-start.1
  1.3 0.1 collective-permute-start
  1.4 2.6 %collective-permute-start.1 = (bf16[6,32,2304]{2,1,0:T(8,128)(2,1)S(1)}, bf16[6,32,2304]{2,1,0:T(8,128)(2,1)S(1)}, u32[]{:S(2)}, u32[]{:S(2)}) collective-permute-start(bf16[6,32,2304]{2,1,0:T(8,128)(2,1)S(1)} %bitcast.16), channel_id=1, source_target_pairs={{0,1},{1,2},{2,3},{3,0},{4,5},{5,6},{6,7},{7,4},{8,9},{9,10},{10,1... | collective-permute-start | bytes 2654216 | tf_op jit(solution)/shard_map/ppermute | solution.py:29
  4.0 0.9 slice.15
  4.9 0.5 collective-permute-start.2
  5.4 0.8 slice_bitcast_fusion.1
  6.2 0.7 fusion.23
  6.9 0.0 copy-start.2
  6.9 15.1 %reshape.103.l_ref = bf16[256,13824]{1,0:T(8,128)(2,1)} reshape(bf16[256,3,2,1,2304]{4,2,3,1,0:T(2,128)(2,1)} %bitcast.13) | data formatting | bytes 14155776 | tf_op jit(solution)/shard_map/reshape | solution.py:408
  22.0 0.0 copy-done.1
  22.0 1.5 %fusion.11 = (f32[16,2304]{1,0:T(8,128)}, f32[16,2304]{1,0:T(8,128)}) fusion(s32[2304]{0:T(1024)S(1)} %get-tuple-element.9, s32[16]{0:T(128)S(1)} %get-tuple-element.8, s32[2304]{0:T(1024)S(1)} %get-tuple-element.10, s32[16]{0:T(128)S(1)} %get-tuple-element.7, f32[16]{0:T(128)S(1)} %fusion.23), kind=kLoop, calls=%fused_computation.15 | loop fusion | flops 700416 | bytes 313536 | tf_op jit(solution)/shard_map/sin | solution.py:92
  23.5 0.0 copy-done.2
  23.5 1.7 %collective-permute-done.2.back_ref = f32[18,1,2304]{2,1,0:T(1,128)S(1)} collective-permute-done((f32[18,1,2304]{2,1,0:T(1,128)S(1)}, f32[18,1,2304]{2,1,0:T(1,128)S(1)}, u32[]{:S(2)}, u32[]{:S(2)}) %collective-permute-start.2) | collective-permute-done | bytes 165920 | tf_op jit(solution)/shard_map/ppermute | solution.py:29
  25.2 0.0 collective-permute-done.plus_ref
  25.2 0.0 collective-permute-done.1.minus_ref
  25.2 0.0 copy-start.4
  25.2 0.6 copy-done.5
  25.9 0.4 copy-done.3
  26.2 0.3 copy-done.4
  26.5 81.0 %shard_map.55.refs_0_ = f32[2,4,128,256]{3,2,1,0:T(8,128)} custom-call(bf16[6,32,2304]{2,1,0:T(8,128)(2,1)} %bitcast.17, bf16[6,32,2304]{2,1,0:T(8,128)(2,1)} %copy-done.3, bf16[6,32,2304]{2,1,0:T(8,128)(2,1)} %copy-done.4, f32[54,1,2304]{2,1,0:T(1,128)} %bitcast.19, f32[18,1,2304]{2,1,0:T(1,128)} %copy-done.5, f32[16,2304]{1,0:T(8,128)} %get-tuple-element.6.cos_ref, ...), custom_call_target="tpu_custom_call" | custom-call | flops 30000001024 | bytes 20000000 | tf_op jit(solution)/shard_map/pallas_call | solution.py:416
  107.5 0.0 copy-start
  107.5 1.2 %copy-done = f32[2,4,128,256]{3,2,1,0:T(8,128)S(1)} copy-done((f32[2,4,128,256]{3,2,1,0:T(8,128)S(1)}, f32[2,4,128,256]{3,2,1,0:T(8,128)}, u32[]{:S(2)}) %copy-start) | copy-done | bytes 1048600
  108.8 1.4 %shard_map.56 = f32[4,2,256,128]{3,2,1,0:T(8,128)} custom-call(f32[2,4,128,256]{3,2,1,0:T(8,128)S(1)} %copy-done, bf16[128,128]{1,0:T(8,128)(2,1)S(1)} %fusion.13.refs_1_), custom_call_target="tpu_custom_call" | custom-call | tf_op jit(solution)/shard_map/pallas_call | solution.py:441
  (4 shorter events, 0.0 us)
Async XLA Ops:
  1.3 20.7 %copy-start.1 = (bf16[3,2,1,32,2304]{4,3,1,0,2:T(8,128)(2,1)}, bf16[3,2,1,32,2304]{4,3,1,0,2:T(8,128)(2,1)S(1)}, u32[]{:S(2)}) copy-start(bf16[3,2,1,32,2304]{4,3,1,0,2:T(8,128)(2,1)S(1)} %copy.6) | copy-start | bytes 2654212
  1.3 23.9 %collective-permute-start = (bf16[6,32,2304]{2,1,0:T(8,128)(2,1)S(1)}, bf16[6,32,2304]{2,1,0:T(8,128)(2,1)S(1)}, u32[]{:S(2)}, u32[]{:S(2)}) collective-permute-start(bf16[6,32,2304]{2,1,0:T(8,128)(2,1)S(1)} %bitcast.15), channel_id=1, source_target_pairs={{0,3},{1,0},{2,1},{3,2},{4,7},{5,4},{6,5},{7,6},{8,11},{9,8},{10,9... | collective-permute-start | bytes 2654216 | tf_op jit(solution)/shard_map/ppermute | solution.py:29
  1.4 23.8 %collective-permute-start.1 = (bf16[6,32,2304]{2,1,0:T(8,128)(2,1)S(1)}, bf16[6,32,2304]{2,1,0:T(8,128)(2,1)S(1)}, u32[]{:S(2)}, u32[]{:S(2)}) collective-permute-start(bf16[6,32,2304]{2,1,0:T(8,128)(2,1)S(1)} %bitcast.16), channel_id=1, source_target_pairs={{0,1},{1,2},{2,3},{3,0},{4,5},{5,6},{6,7},{7,4},{8,9},{9,10},{10,1... | collective-permute-start | bytes 2654216 | tf_op jit(solution)/shard_map/ppermute | solution.py:29
  4.9 20.3 %collective-permute-start.2 = (f32[18,1,2304]{2,1,0:T(1,128)S(1)}, f32[18,1,2304]{2,1,0:T(1,128)S(1)}, u32[]{:S(2)}, u32[]{:S(2)}) collective-permute-start(f32[18,1,2304]{2,1,0:T(1,128)S(1)} %bitcast.18), channel_id=1, source_target_pairs={{0,1},{1,2},{2,3},{3,0},{4,5},{5,6},{6,7},{7,4},{8,9},{9,10},{10,1... | collective-permute-start | bytes 497672 | tf_op jit(solution)/shard_map/ppermute | solution.py:29
  6.9 16.6 %copy-start.2 = (s32[128]{0:T(128)S(1)}, s32[128]{0:T(128)}, u32[]{:S(2)}) copy-start(s32[128]{0:T(128)} %param.9) | copy-start | bytes 1540
  25.2 0.7 copy-start.5
  25.2 1.0 copy-start.3
  25.2 1.4 %copy-start.4 = (bf16[6,32,2304]{2,1,0:T(8,128)(2,1)}, bf16[6,32,2304]{2,1,0:T(8,128)(2,1)S(1)}, u32[]{:S(2)}) copy-start(bf16[6,32,2304]{2,1,0:T(8,128)(2,1)S(1)} %collective-permute-done.1.minus_ref) | copy-start | bytes 2654212
  107.5 1.2 %copy-start = (f32[2,4,128,256]{3,2,1,0:T(8,128)S(1)}, f32[2,4,128,256]{3,2,1,0:T(8,128)}, u32[]{:S(2)}) copy-start(f32[2,4,128,256]{3,2,1,0:T(8,128)} %shard_map.55.refs_0_) | copy-start | bytes 3145732
